TPU v7x, 32 devices: a whole 2x2x4 slice. The times are simulated.
32 devices in a mesh: gz: 16 (over z, x, core), xy: 2 (over y).
Axes of the slice: x: 2, y: 2, z: 4, core: 2. Of those that a mesh axis runs over, the one named last changes fastest.
Arguments:
- moments: bfloat16 [361, 128, 256], P(None, 'gz', 'xy'), may hold values from -4 to 4
- counts: int32 [128, 256], P('gz', 'xy'), may hold values from 0 to 7
- m2x: bfloat16 [1296, 361], replicated, may hold values from -0.3125 to 0.3125
- x2l: bfloat16 [361, 1296], replicated, may hold values from -0.0625 to 0.0625
- decay_rate: float32 [648], replicated, may hold values from 0.001953125 to 0.05
- wave_x: float32 [648], replicated, may hold values from -3.140625 to 3.140625
- wave_y: float32 [648], replicated, may hold values from -3.140625 to 3.140625
- offsets: int32 [6, 2], replicated, may hold values from -2 to 2, as said below
Outputs:
- local_out: bfloat16 [361, 128, 256], P(None, 'gz', 'xy')
Inputs may be any that keep to these rules, and one draw needn't show every extreme that they name: `offsets`: some row is (2, -2) and some row is (-2, 2).
All inputs are finite; a program needn't handle non-finite values.
Results may differ from a plain program's by a relative error of at most 0.0064.
Values may be sent and summed in bfloat16 or wider, within the bound.
A program may use at most 192 MiB of HBM per device.

v0:
```python
import jax
import jax.numpy as jnp
from jax import lax
from jax.sharding import PartitionSpec as P

BY = 8
R = 2
NOFF = 6


def from_behind(value, axis, steps):
    count = lax.axis_size(axis)
    pairs = [(source, (source + steps) % count) for source in range(count)]
    return lax.ppermute(value, axis, pairs)


def entering_2(part, axis, combine, identity):
    place = lax.axis_index(axis)
    gathered = jax.tree.map(lambda a: lax.all_gather(a, axis), part)
    state = jax.tree.map(lambda a, e: jnp.zeros_like(a) + jnp.asarray(e, a.dtype), part, identity)

    def one(turn, state):
        return combine(
            state, jax.tree.map(lambda a: lax.dynamic_index_in_dim(a, turn, 0, False), gathered)
        )

    return lax.fori_loop(0, place, one, state)


def extended(block, sides, width):
    for axis, dim in sides:
        count = lax.axis_size(axis)
        forward = [(i, i + 1) for i in range(count - 1)]
        forward.append((count - 1, 0))
        backward = [(target, source) for source, target in forward]
        low = lax.ppermute(
            lax.slice_in_dim(block, block.shape[dim] - width, None, axis=dim), axis, forward
        )
        high = lax.ppermute(lax.slice_in_dim(block, 0, width, axis=dim), axis, backward)
        block = jnp.concatenate([low, block, high], axis=dim)
    return block


def build_upward(box_terms, entering, before_term, rate_col, factor):
    layers = box_terms.shape[1]
    layer_pos = jnp.arange(layers, dtype=jnp.float32)
    layer_gap = layer_pos[:, None] - layer_pos[None, :]
    decay_table = jnp.where(
        layer_gap[None] >= 2.0,
        jnp.exp(-rate_col[:, :, None] * jnp.maximum(layer_gap, 0.0)[None]),
        0.0,
    )
    upward = jnp.einsum("kij,kjb->kib", decay_table, box_terms, precision=lax.Precision.HIGHEST)
    upward = (
        upward + jnp.exp(-rate_col * (layer_pos + 1.0)[None, :])[:, :, None] * entering[:, None, :]
    )
    upward = upward.at[:, 0, :].add(-factor * before_term)
    return upward


def body(moments, counts, m2x, x2l, decay_rate, wave_x, wave_y, offsets):
    coeffs, layers, plane_size = moments.shape
    exp_rows = m2x.shape[0]
    half_rows = exp_rows // 2
    columns = plane_size // BY
    loop_size = lax.axis_size("gz")
    slab_pos = lax.axis_index("gz").astype(jnp.float32)
    rate_col = jnp.concatenate([decay_rate, decay_rate])[:, None]
    factor = jnp.exp(-rate_col)
    weight = jnp.sqrt(1.0 - factor * factor)
    multipole = (moments.astype(jnp.float32) * counts.astype(jnp.float32)[None]).astype(
        jnp.bfloat16
    )
    expansion = jnp.dot(
        m2x, multipole.reshape(coeffs, layers * plane_size), preferred_element_type=jnp.float32
    )
    box_terms = (weight * expansion).reshape(exp_rows, layers, plane_size)
    layer_pos = jnp.arange(layers, dtype=jnp.float32)
    tail_power = jnp.exp(-rate_col * (layers - 1.0 - layer_pos)[None, :])
    outgoing = jnp.einsum("kz,kzb->kb", tail_power, box_terms, precision=lax.Precision.HIGHEST)
    before_term = from_behind(box_terms[:, layers - 1, :].astype(jnp.bfloat16), "gz", 1).astype(
        jnp.float32
    )
    slab_decay = jnp.exp(-rate_col * layers)
    lap_gain = 1.0 - jnp.exp(-rate_col * (layers * loop_size))

    def combine(earlier, later):
        return (earlier[0] * later[0], later[0] * earlier[1] + later[1])

    identity = (jnp.ones_like(slab_decay), jnp.zeros_like(outgoing))
    _, prefix = entering_2((slab_decay, outgoing), "gz", combine, identity)
    scaled = jnp.exp(-rate_col * (layers * (loop_size - 1.0 - slab_pos))) * outgoing
    lap_sum = lax.psum(scaled, "gz")
    entering = prefix + jnp.exp(-rate_col * (layers * slab_pos)) * lap_sum / lap_gain
    upward = build_upward(box_terms, entering, before_term, rate_col, factor)
    field_grid = upward.astype(jnp.bfloat16).reshape(exp_rows, layers, columns, BY)
    padded = extended(field_grid, (("xy", 2),), R)
    acc_real = jnp.zeros((half_rows, layers, columns, BY), jnp.float32)
    acc_imag = jnp.zeros((half_rows, layers, columns, BY), jnp.float32)
    for list_entry in range(NOFF):
        step_x = offsets[list_entry, 0]
        step_y = offsets[list_entry, 1]
        moved = lax.dynamic_slice_in_dim(padded, R - step_x, columns, 2)
        moved = jnp.roll(moved, step_y, axis=3)
        phase_angle = wave_x * step_x.astype(jnp.float32) + wave_y * step_y.astype(jnp.float32)
        cosine = jnp.cos(phase_angle)[:, None, None, None]
        sine_part = jnp.sin(phase_angle)[:, None, None, None]
        part_real = moved[:half_rows].astype(jnp.float32)
        part_imag = moved[half_rows:].astype(jnp.float32)
        acc_real = acc_real + part_real * cosine - part_imag * sine_part
        acc_imag = acc_imag + part_real * sine_part + part_imag * cosine
    shifted = (
        jnp.concatenate([acc_real, acc_imag], axis=0)
        .astype(jnp.bfloat16)
        .reshape(exp_rows, layers * plane_size)
    )
    local_out = jnp.dot(x2l, shifted, preferred_element_type=jnp.float32).astype(jnp.bfloat16)
    return local_out.reshape(coeffs, layers, plane_size)


def solution(mesh):
    in_specs = (P(None, "gz", "xy"), P("gz", "xy"), P(), P(), P(), P(), P(), P())
    out_specs = P(None, "gz", "xy")
    return jax.shard_map(body, mesh=mesh, in_specs=in_specs, out_specs=out_specs, check_vma=False)
```

profile of v0, /device:TPU:0, one launch (start us, length us, event | category | flops | bytes accessed | tf_op | source)
XLA Modules:
  0.0 327.6 jit_solution(16185652126443891550)
XLA Ops:
  6.6 0.9 exponential_negate_fusion
  7.5 0.8 copy.17
  9.1 1.3 multiply_convert_fusion
  10.6 1.6 multiply_bitcast_fusion
  12.2 1.3 copy.22
  13.5 9.6 %fusion.68 = f32[1296,1,128]{2,1,0:T(1,128)} fusion(f32[1296,8,1]{1,2,0:T(1,128)S(1)} %copy.17, f32[1296,8,128]{2,1,0:T(8,128)S(1)} %bitcast.59), kind=kOutput, calls=%fused_computation.135 | convolution fusion | flops 15925248 | bytes 6013440 | tf_op jit(solution)/shard_map/kz,kzb->kb/dot_general | solution.py:80
  23.1 2.9 slice.133
  26.6 1.1 broadcast_multiply_fusion
  28.1 23.6 %all_gather.10 = f32[16,1296,1]{1,2,0:T(1,128)S(1)} all-gather(f32[1,1296,1]{1,2,0:T(1,128)S(1)} %fusion.49), channel_id=1, replica_groups=mesh['gz'=16,'xy'=2] {'gz'}, dimensions={0}, use_global_device_ids=true | all-gather | bytes 88128 | tf_op jit(solution)/shard_map/all_gather | solution.py:19
  51.9 63.0 %all-gather.3.cloned.1.call-done = f32[20736,128]{1,0:T(8,128)} async-done(((f32[1296,128]{1,0:T(8,128)}), f32[20736,128]{1,0:T(8,128)}) %all-gather.3.cloned.1.call-update) | async-done | bytes 10616848 | tf_op jit(solution)/shard_map/all_gather | solution.py:19
  115.2 92.6 %all-reduce.2.cloned.1.call-done = f32[1296,128]{1,0:T(8,128)} async-done(((f32[1296,128]{1,0:T(8,128)}), f32[1296,128]{1,0:T(8,128)}) %all-reduce.2.cloned.1.call-update) | async-done | bytes 663568 | tf_op jit(solution)/shard_map/psum | solution.py:93
  207.8 1.5 divide_add_fusion
  209.3 13.8 %multiply_add_fusion = f32[1296,8,128]{2,1,0:T(8,128)S(1)} fusion(f32[1296,128]{1,0:T(8,128)S(1)} %divide_add_fusion, f32[1296,8]{1,0:T(8,128)S(1)} %copy.14, f32[1296,8,128]{2,1,0:T(8,128)} %bitcast.61, f32[8,8]{1,0:T(8,128)S(1)} %fusion.50, f32[1296]{0:T(1024)S(1)} %get-tuple-element.100, pred[8,8]{1,0:T(8,128)(4,1)S(1)} %fusion.51), kind=kOutput, calls=%fused_computation.14 | convolution fusion | flops 130222080 | bytes 11327360 | tf_op jit(solution)/shard_map/kij,kjb->kib/dot_general | solution.py:53
  223.1 2.4 copy-done.3
  225.5 0.7 slice_add_fusion
  226.3 18.9 %scatter-add.4 = f32[1296,8,128]{2,1,0:T(8,128)} dynamic-update-slice(f32[1296,8,128]{2,1,0:T(8,128)} %copy-done.3, f32[1296,1,128]{2,1,0:T(1,128)S(1)} %slice_add_fusion, s32[]{:T(128)} %constant.97.clone.1, s32[]{:T(128)} %constant.97.clone.1, s32[]{:T(128)} %constant.97.clone.1) | dynamic-update-slice | bytes 1327108 | tf_op jit(solution)/shard_map/scatter-add | solution.py:57
  245.1 3.8 %convert_element_type.126 = bf16[1296,8,128]{2,1,0:T(8,128)(2,1)} convert(f32[1296,8,128]{2,1,0:T(8,128)} %scatter-add.4) | non-fusion elementwise | flops 1327104 | bytes 7962624 | tf_op jit(solution)/shard_map/convert_element_type | solution.py:96
  248.9 4.9 %copy.16 = bf16[1296,8,128]{0,2,1:T(8,128)(2,1)} copy(bf16[1296,8,128]{2,1,0:T(8,128)(2,1)} %convert_element_type.126) | data formatting | bytes 5308416 | tf_op jit(solution)/shard_map/convert_element_type | solution.py:96
  253.8 1.1 fusion.66
  254.9 1.5 collective-permute-start.1
  283.5 2.1 pad_maximum_fusion
  285.6 3.3 %constant_dynamic-slice_fusion.5 = (bf16[1296,8,16,8]{0,3,2,1:T(8,128)(2,1)S(1)}, bf16[1296,8,16,8]{0,3,2,1:T(8,128)(2,1)S(1)}, bf16[1296,8,16,8]{0,3,2,1:T(8,12...) fusion(bf16[1296,8,20,8]{0,3,2,1:T(8,128)(2,1)S(1)} %pad_maximu, ...), kind=kLoop, calls=%fused_computation.107 | loop fusion | bytes 31850520 | tf_op jit(solution)/shard_map/dynamic_slice | solution.py:103
  288.9 4.7 %fusion.29 = bf16[1296,8,16,8]{0,3,2,1:T(8,128)(2,1)S(1)} fusion(s32[]{:T(128)S(6)} %select_n.65, bf16[1296,8,16,8]{0,3,2,1:T(8,128)(2,1)} %get-tuple-element.75), kind=kLoop, calls=%fused_computation.70 | loop fusion | flops 5308416 | bytes 5308420 | tf_op jit(solution)/shard_map/jit(_roll_dynamic)/concatenate | solution.py:104
  293.6 2.1 fusion.30
  295.6 2.1 fusion.31
  297.7 2.1 fusion.32
  299.8 2.1 fusion.33
  301.9 2.3 fusion.28
  304.1 7.1 %fusion.15 = bf16[648,8,16,8]{0,3,2,1:T(8,128)(2,1)S(1)} fusion(f32[648]{0:T(1024)S(1)} %get-tuple-element.84, f32[648]{0:T(1024)S(1)} %get-tuple-element.93, f32[648]{0:T(1024)S(1)} %get-tuple-element.85, f32[648]{0:T(1024)S(1)} %get-tuple-element.94, f32[648]{0:T(1024)S(1)} %get-tuple-element.86, f32[648]{0:T(1024)S(1)} %get-tuple-element.90, ...), kind=kLoop, calls=%fused_computation.56 | loop fusion | flops 23887872 | bytes 17283456 | tf_op jit(solution)/shard_map/convert.3
  311.2 6.9 %fusion.27 = bf16[648,8,16,8]{0,3,2,1:T(8,128)(2,1)S(1)} fusion(f32[648]{0:T(1024)S(1)} %get-tuple-element.84, f32[648]{0:T(1024)S(1)} %get-tuple-element.93, f32[648]{0:T(1024)S(1)} %get-tuple-element.85, f32[648]{0:T(1024)S(1)} %get-tuple-element.94, f32[648]{0:T(1024)S(1)} %get-tuple-element.86, f32[648]{0:T(1024)S(1)} %get-tuple-element.90, ...), kind=kLoop, calls=%fused_computation.68 | loop fusion | flops 23887872 | bytes 17283456 | tf_op jit(solution)/shard_map/convert.2
  318.2 1.5 fusion.44
  319.8 0.9 slice.148
  (45 shorter events, 4.0 us)
Async XLA Ops:
  6.5 4.0 %copy-start = (bf16[1296,361]{1,0:T(8,128)(2,1)S(1)}, bf16[1296,361]{1,0:T(8,128)(2,1)}, u32[]{:S(2)}) copy-start(bf16[1296,361]{1,0:T(8,128)(2,1)} %param.16) | copy-start | bytes 2807140
  6.5 108.4 %all-gather.3.cloned.1.call-start = ((), (), s32[]{:S(2)}) async-start(), calls=%async_computation.1 | async-start | bytes 11280384 | tf_op jit(solution)/shard_map/all_gather | solution.py:19
  13.5 9.6 %copy-start.2 = (f32[162,8,8,128]{3,2,1,0:T(8,128)}, f32[162,8,8,128]{3,2,1,0:T(8,128)S(1)}, u32[]{:S(2)}) copy-start(f32[162,8,8,128]{3,2,1,0:T(8,128)S(1)} %copy.22) | copy-start | bytes 15925252
  23.0 3.6 %copy-start.4 = (f32[1296,1,128]{2,1,0:T(1,128)S(1)}, f32[1296,1,128]{2,1,0:T(1,128)}, u32[]{:S(2)}) copy-start(f32[1296,1,128]{2,1,0:T(1,128)} %fusion.68) | copy-start | bytes 1990660
  23.1 4.7 %copy-start.6 = (f32[648]{0:T(1024)S(1)}, f32[648]{0:T(1024)}, u32[]{:S(2)}) copy-start(f32[648]{0:T(1024)} %param.18) | copy-start | bytes 7780
  23.1 184.7 %all-reduce.2.cloned.1.call-start = ((), (), s32[]{:S(2)}) async-start(), calls=%async_computation | async-start | bytes 1327104 | tf_op jit(solution)/shard_map/psum | solution.py:93
  26.1 25.6 %collective-permute-start = (bf16[1296,128]{1,0:T(8,128)(2,1)S(1)}, bf16[1296,128]{1,0:T(8,128)(2,1)S(1)}, u32[]{:S(2)}, u32[]{:S(2)}) collective-permute-start(bf16[1296,128]{1,0:T(8,128)(2,1)S(1)} %bitcast.74), channel_id=1, source_target_pairs={{0,2},{2,4},{4,6},{6,8},{8,10},{10,12},{12,14},{14,16},{16,18},{18... | collective-permute-start | bytes 995336 | tf_op jit(solution)/shard_map/ppermute | solution.py:14
  223.1 2.4 copy-start.3
  248.9 8.1 %copy-start.5 = (s32[6,2]{0,1:T(2,128)S(1)}, s32[6,2]{0,1:T(2,128)}, u32[]{:S(2)}) copy-start(s32[6,2]{0,1:T(2,128)} %param.21) | copy-start | bytes 148
  248.9 34.4 %copy-start.7 = (f32[648]{0:T(1024)S(1)}, f32[648]{0:T(1024)}, u32[]{:S(2)}) copy-start(f32[648]{0:T(1024)} %param.20) | copy-start | bytes 7780
  248.9 34.4 %copy-start.8 = (f32[648]{0:T(1024)S(1)}, f32[648]{0:T(1024)}, u32[]{:S(2)}) copy-start(f32[648]{0:T(1024)} %param.19) | copy-start | bytes 7780
  254.9 28.5 %collective-permute-start.1 = (bf16[1296,8,2,8]{0,3,2,1:T(8,128)(2,1)S(1)}, bf16[1296,8,2,8]{0,3,2,1:T(8,128)(2,1)S(1)}, u32[]{:S(2)}, u32[]{:S(2)}) collective-permute-start(bf16[1296,8,2,8]{0,3,2,1:T(8,128)(2,1)S(1)} %get-tuple-element.79), channel_id=1, source_target_pairs={{0,1},{1,0},{2,3},{3,2},{4,5},{5,4},{6,7},{7,6},{8,9},{9,8},{10,11... | collective-permute-start | bytes 995336 | tf_op jit(solution)/shard_map/ppermute | solution.py:36
  256.5 27.0 %collective-permute-start.2 = (bf16[1296,8,2,8]{0,3,2,1:T(8,128)(2,1)S(1)}, bf16[1296,8,2,8]{0,3,2,1:T(8,128)(2,1)S(1)}, u32[]{:S(2)}, u32[]{:S(2)}) collective-permute-start(bf16[1296,8,2,8]{0,3,2,1:T(8,128)(2,1)S(1)} %get-tuple-element.80), channel_id=1, source_target_pairs={{1,0},{0,1},{3,2},{2,3},{5,4},{4,5},{7,6},{6,7},{9,8},{8,9},{11,10... | collective-permute-start | bytes 995336 | tf_op jit(solution)/shard_map/ppermute | solution.py:39
  311.2 7.0 %copy-start.9 = (bf16[361,1296]{0,1:T(8,128)(2,1)S(1)}, bf16[361,1296]{0,1:T(8,128)(2,1)}, u32[]{:S(2)}) copy-start(bf16[361,1296]{0,1:T(8,128)(2,1)} %param.17) | copy-start | bytes 2807140
  318.2 2.6 copy-start.1
Sparse Core Ops, SparseCore 0:
  23.2 91.7 all-gather.2
  118.4 89.3 all-reduce.1
where the time goes:
time: 329 us; the launch traced here: 328 us
  waiting for transfers between devices  156 us (47%)
  other arithmetic  41.8 us (13%)
  between operations  39.3 us (12%)
  local copies, waits for them, and re-layouts  38 us (12%)
  matrix products  26.5 us (8%)
  blocking collectives  23.6 us (7%)
    psum x1, waiting for transfers between devices, body(): lap_sum = lax.psum(scaled, 'gz')  92.6 us
    all_gather x1, waiting for transfers between devices, entering_2(): gathered = jax.tree.map(lambda a: lax.all_gather(a, axis), part)  63 us
    all_gather x1, blocking collectives, entering_2(): gathered = jax.tree.map(lambda a: lax.all_gather(a, axis), part)  23.6 us
    scatter-add x1, local copies, waits for them, and re-layouts, build_upward(): upward = upward.at[:, 0, :].add(-factor * before_term)  18.9 us
    concatenate x6, other arithmetic, body(): moved = jnp.roll(moved, step_y, axis=3)  15.2 us
    another operation x2, other arithmetic  14 us
    dot_general x1, matrix products, build_upward(): jnp.einsum('kij,kjb->kib', decay_table, box_terms, precision=lax.Precisio...  13.8 us
    dot_general x1, matrix products, body(): jnp.einsum('kz,kzb->kb', tail_power, box_terms, precision=lax.Precision.H...  9.58 us
  transfers between devices with their start and end apart: 5, of which 2 were waited for; matrix products, arithmetic and copies ran while one was open for 2% of the time, Pallas kernels for 0%

commit v1 on v0

v1 whole, which is shorter than its diff:
```python
import functools

import jax
import jax.numpy as jnp
from jax import lax
from jax.experimental import pallas as pl
from jax.experimental.pallas import tpu as pltpu
from jax.sharding import PartitionSpec as P

BY = 8
R = 2
NOFF = 6
GROUP = 4
BOXES = 128
MESH = pl.DeviceIdType.MESH
F32 = jnp.float32
BF16 = jnp.bfloat16


def up(value, step):
    return -(-value // step) * step


def kernel(
    loop_size, layers, rows,
    off_ref, mp_ref, m2x_ref, xs_ref, cs_ref, rate_ref,
    out_ref,
    terms, outgo, top, below, ingroup, planes, entbuf, enter, wall, upward, perm, place, mixed,
    own, edge, edge_out, edge_in,
    top_s, top_r, a_s, a_r, b_s, b_r, c_s, c_r, e_s, e_r,
):
    slab = lax.axis_index("gz")
    half = lax.axis_index("xy")
    groups = loop_size // GROUP
    group, member = slab // GROUP, lax.rem(slab, GROUP)
    after = lax.rem(slab + 1, loop_size)
    before = lax.rem(slab + loop_size - 1, loop_size)
    padded = outgo.shape[0]
    quarter = padded // GROUP
    out_rows = out_ref.shape[0]
    coeffs = m2x_ref.shape[1]

    def mate(step):
        return lax.rem(member + step, GROUP)

    def mate_id(step):
        return group * GROUP + mate(step)

    def plane_id(step):
        return lax.rem(group + step, groups) * GROUP + member

    barrier = pltpu.get_barrier_semaphore()
    partners = [after, before]
    partners += [mate_id(step) for step in range(1, GROUP)]
    partners += [plane_id(step) for step in range(1, groups)]
    for partner in partners:
        pl.semaphore_signal(barrier, inc=1, device_id={"gz": partner}, device_id_type=MESH)
    pl.semaphore_signal(barrier, inc=1, device_id={"xy": 1 - half}, device_id_type=MESH)
    pl.semaphore_wait(barrier, len(partners) + 1)

    top_copy = pltpu.make_async_remote_copy(
        src_ref=mp_ref.at[:, pl.ds((layers - 1) * BOXES, BOXES)],
        dst_ref=top, send_sem=top_s, recv_sem=top_r,
        device_id={"gz": after}, device_id_type=MESH,
    )
    top_copy.start()

    block = rows // 3

    @pl.loop(0, 3)
    def _(turn):
        at = pl.ds(pl.multiple_of(turn * block, 16), block)
        terms[at, :] = jnp.dot(m2x_ref[at, :], mp_ref[0:coeffs, :], preferred_element_type=F32)

    @pl.loop(0, rows // 16)
    def _(turn):
        at = pl.ds(pl.multiple_of(turn * 16, 16), 16)
        factor = jnp.exp(-rate_ref[at, :])
        square = factor * factor
        weight = jnp.sqrt(1.0 - square)
        box = [weight * terms[at, z * BOXES:(z + 1) * BOXES] for z in range(layers)]
        total = box[0]
        for z in range(1, layers):
            total = factor * total + box[z]
        outgo[at, :] = total.astype(BF16)
        state = jnp.zeros_like(factor)
        for z in range(2, layers):
            state = factor * state + square * box[z - 2]
            terms[at, z * BOXES:(z + 1) * BOXES] = state

    outgo[rows:padded, :] = jnp.zeros((padded - rows, BOXES), BF16)

    a_copies = []
    for step in range(1, GROUP):
        copy = pltpu.make_async_remote_copy(
            src_ref=outgo.at[pl.ds(pl.multiple_of(mate(step) * quarter, 16), quarter), :],
            dst_ref=ingroup.at[step], send_sem=a_s.at[step], recv_sem=a_r.at[step],
            device_id={"gz": mate_id(step)}, device_id_type=MESH,
        )
        copy.start()
        a_copies.append(copy)
    mine = pl.ds(pl.multiple_of(member * quarter, 16), quarter)
    ingroup[0] = outgo[mine, :]

    @pl.loop(0, out_rows // 16)
    def _(turn):
        real = xs_ref[pl.ds(pl.multiple_of(turn * 16, 16), 16), :].astype(F32)
        swap = xs_ref[pl.ds(pl.multiple_of(out_rows + turn * 16, 16), 16), :].astype(F32)
        for entry in range(NOFF):
            mix = real * cs_ref[entry:entry + 1, :] + swap * cs_ref[8 + entry:9 + entry, :]
            wall[pl.ds(pl.multiple_of(entry * out_rows + turn * 16, 16), 16), :] = mix.astype(BF16)

    lane = lax.broadcasted_iota(jnp.int32, (BOXES, 2 * BOXES), 0)
    column = lax.broadcasted_iota(jnp.int32, (BOXES, 2 * BOXES), 1)
    width = BOXES // BY
    for entry in range(NOFF):
        moved_x = lane // BY + off_ref[entry, 0]
        moved_y = (lane + off_ref[entry, 1]) & (BY - 1)
        inside = moved_x * BY + moved_y
        low = (moved_x + R) * BY + moved_y + BOXES
        high = (moved_x - width + R) * BY + moved_y + BOXES
        stays = (moved_x >= 0) & (moved_x < width)
        outside = jnp.where(moved_x < 0, low, high)
        for slot in range(4):
            target = jnp.where(stays, inside, outside + slot * 2 * R * BY)
            perm[slot, entry * BOXES:(entry + 1) * BOXES, :] = jnp.where(
                column == target, 1.0, 0.0).astype(BF16)
    lane = lax.broadcasted_iota(jnp.int32, (BOXES, BOXES), 0)
    column = lax.broadcasted_iota(jnp.int32, (BOXES, BOXES), 1)
    for slot in range(4):
        inner = lane - slot * 2 * R * BY
        target = jnp.where(inner < R * BY, inner + BOXES - R * BY, inner - R * BY)
        hit = (inner >= 0) & (inner < 2 * R * BY) & (column == target)
        place[slot] = jnp.where(hit, 1.0, 0.0).astype(BF16)

    for copy in a_copies:
        copy.wait_recv()

    def source(index):
        return ingroup[lax.rem(member - index + GROUP, GROUP)].astype(F32)

    rate = rate_ref[mine, :]
    decay = jnp.exp(-rate * layers)
    total = source(0)
    for index in range(1, GROUP):
        total = decay * total + source(index)
    planes[0] = total.astype(BF16)
    b_copies = []
    for step in range(1, groups):
        copy = pltpu.make_async_remote_copy(
            src_ref=planes.at[0],
            dst_ref=planes.at[step], send_sem=b_s.at[step], recv_sem=b_r.at[step],
            device_id={"gz": plane_id(step)}, device_id_type=MESH,
        )
        copy.start()
        b_copies.append(copy)

    top_copy.wait_recv()

    @pl.loop(0, 3)
    def _(turn):
        at = pl.ds(pl.multiple_of(turn * block, 16), block)
        below[at, :] = jnp.dot(m2x_ref[at, :], top[0:coeffs, :], preferred_element_type=F32)

    for copy in b_copies:
        copy.wait_recv()
    plane_decay = jnp.exp(-rate * (layers * GROUP))
    total = planes[0].astype(F32)
    for step in range(groups - 1, 0, -1):
        total = plane_decay * total + planes[step].astype(F32)
    state = total / (1.0 - jnp.exp(-rate * (layers * loop_size)))
    entbuf[0] = state.astype(BF16)
    for index in range(1, GROUP):
        state = decay * state + source(index - 1)
        entbuf[index] = state.astype(BF16)

    c_copies = []
    for step in range(1, GROUP):
        copy = pltpu.make_async_remote_copy(
            src_ref=entbuf.at[mate(step)],
            dst_ref=enter.at[mine, :],
            send_sem=c_s.at[step], recv_sem=c_r.at[step],
            device_id={"gz": mate_id(step)}, device_id_type=MESH,
        )
        copy.start()
        c_copies.append(copy)
    enter[mine, :] = entbuf[member]
    for step in range(1, GROUP):
        sender = lax.rem(member - step + GROUP, GROUP)
        pltpu.make_async_remote_copy(
            src_ref=entbuf.at[0],
            dst_ref=enter.at[pl.ds(pl.multiple_of(sender * quarter, 16), quarter), :],
            send_sem=c_s.at[step], recv_sem=c_r.at[step],
            device_id={"gz": mate_id(step)}, device_id_type=MESH,
        ).wait_recv()

    @pl.loop(0, rows // 16)
    def _(turn):
        at = pl.ds(pl.multiple_of(turn * 16, 16), 16)
        factor = jnp.exp(-rate_ref[at, :])
        weight = jnp.sqrt(1.0 - factor * factor)
        state = factor * enter[at, :].astype(F32)
        upward[at, 0:BOXES] = (state - factor * (weight * below[at, :])).astype(BF16)
        state = factor * state
        upward[at, BOXES:2 * BOXES] = state.astype(BF16)
        for z in range(2, layers):
            state = factor * state
            upward[at, z * BOXES:(z + 1) * BOXES] = (
                state + terms[at, z * BOXES:(z + 1) * BOXES]).astype(BF16)

    e_copies = []
    for pair in range(layers // 2):
        @pl.loop(0, NOFF)
        def _(entry):
            part = jnp.dot(
                wall[pl.ds(pl.multiple_of(entry * out_rows, 16), out_rows), :],
                upward[:, pair * 2 * BOXES:(pair + 1) * 2 * BOXES],
                preferred_element_type=F32,
            ).astype(BF16)
            at = pl.ds(pl.multiple_of(entry * BOXES, BOXES), BOXES)
            mixed[0, :, at] = part[:, :BOXES]
            mixed[1, :, at] = part[:, BOXES:]

        for inner in range(2):
            z = pair * 2 + inner
            placed = jnp.dot(mixed[inner], perm[z % 4], preferred_element_type=F32)
            own[:, z * BOXES:(z + 1) * BOXES] = placed[:, :BOXES]
            if z % 4 == 0:
                edge[...] = placed[:, BOXES:]
            else:
                edge[...] += placed[:, BOXES:]
        if pair % 2 == 1:
            side = pair // 2
            edge_out[side] = edge[...].astype(BF16)
            copy = pltpu.make_async_remote_copy(
                src_ref=edge_out.at[side], dst_ref=edge_in.at[side],
                send_sem=e_s.at[side], recv_sem=e_r.at[side],
                device_id={"xy": 1 - half}, device_id_type=MESH,
            )
            copy.start()
            e_copies.append(copy)

    for side, copy in enumerate(e_copies):
        copy.wait_recv()
        for slot in range(4):
            at = slice((side * 4 + slot) * BOXES, (side * 4 + slot + 1) * BOXES)
            out_ref[:, at] = (
                own[:, at] + jnp.dot(edge_in[side], place[slot], preferred_element_type=F32)
            ).astype(BF16)

    for copy in [top_copy] + a_copies + b_copies + c_copies + e_copies:
        copy.wait_send()


def body(moments, counts, m2x, x2l, decay_rate, wave_x, wave_y, offsets):
    coeffs, layers, plane_size = moments.shape
    rows = m2x.shape[0]
    loop_size = lax.axis_size("gz")
    groups = loop_size // GROUP
    padded = up(rows, 16 * GROUP)
    quarter = padded // GROUP
    in_rows = up(coeffs, 16)
    lanes = layers * plane_size

    multipole = (moments.astype(F32) * counts.astype(F32)[None]).astype(BF16)
    multipole = jnp.pad(multipole.reshape(coeffs, lanes), ((0, in_rows - coeffs), (0, 0)))
    swapped = jnp.concatenate([x2l[:, rows // 2:], x2l[:, :rows // 2]], axis=1)
    spare = ((0, in_rows - coeffs), (0, 0))
    maps = jnp.concatenate([jnp.pad(x2l, spare), jnp.pad(swapped, spare)], axis=0)
    steps = offsets.astype(F32)
    angle = steps[:, :1] * wave_x[None] + steps[:, 1:] * wave_y[None]
    cosine, sine = jnp.cos(angle), jnp.sin(angle)
    gap = jnp.zeros((2, rows), F32)
    phases = jnp.concatenate([
        jnp.concatenate([cosine, cosine], axis=1), gap,
        jnp.concatenate([sine, -sine], axis=1), gap], axis=0)
    rate = jnp.concatenate([decay_rate, decay_rate, jnp.full((padded - rows,), 0.01, F32)])
    rate = jnp.broadcast_to(rate[:, None], (padded, BOXES))

    vmem = pl.BlockSpec(memory_space=pltpu.VMEM)
    dma = pltpu.SemaphoreType.DMA
    out = pl.pallas_call(
        functools.partial(kernel, loop_size, layers, rows),
        out_shape=jax.ShapeDtypeStruct((in_rows, lanes), BF16),
        in_specs=[pl.BlockSpec(memory_space=pltpu.SMEM)] + [vmem] * 5,
        out_specs=vmem,
        scratch_shapes=[
            pltpu.VMEM((rows, lanes), F32),
            pltpu.VMEM((padded, BOXES), BF16),
            pltpu.VMEM((in_rows, BOXES), BF16),
            pltpu.VMEM((rows, BOXES), F32),
            pltpu.VMEM((GROUP, quarter, BOXES), BF16),
            pltpu.VMEM((groups, quarter, BOXES), BF16),
            pltpu.VMEM((GROUP, quarter, BOXES), BF16),
            pltpu.VMEM((padded, BOXES), BF16),
            pltpu.VMEM((NOFF * in_rows, rows), BF16),
            pltpu.VMEM((rows, lanes), BF16),
            pltpu.VMEM((4, NOFF * BOXES, 2 * BOXES), BF16),
            pltpu.VMEM((4, BOXES, BOXES), BF16),
            pltpu.VMEM((2, in_rows, NOFF * BOXES), BF16),
            pltpu.VMEM((in_rows, lanes), F32),
            pltpu.VMEM((in_rows, BOXES), F32),
            pltpu.VMEM((2, in_rows, BOXES), BF16),
            pltpu.VMEM((2, in_rows, BOXES), BF16),
            dma, dma,
            dma((GROUP,)), dma((GROUP,)),
            dma((groups,)), dma((groups,)),
            dma((GROUP,)), dma((GROUP,)),
            dma((2,)), dma((2,)),
        ],
        compiler_params=pltpu.CompilerParams(
            collective_id=0, has_side_effects=True, vmem_limit_bytes=56 * 2**20
        ),
        cost_estimate=pl.CostEstimate(
            flops=16 * rows * coeffs * lanes, bytes_accessed=6 * 2**20, transcendentals=0
        ),
    )(offsets, multipole, m2x, maps, phases, rate)
    return out[:coeffs].reshape(coeffs, layers, plane_size)


def solution(mesh):
    in_specs = (P(None, "gz", "xy"), P("gz", "xy"), P(), P(), P(), P(), P(), P())
    out_specs = P(None, "gz", "xy")
    return jax.shard_map(body, mesh=mesh, in_specs=in_specs, out_specs=out_specs, check_vma=False)
```

time: 329 us -> 61.6 us (0.19)
  waiting for transfers between devices: 156 us -> 0 us
  Pallas kernels: 0 us -> 49.8 us
  between operations: 39.3 us -> 0.11 us
  other arithmetic: 41.8 us -> 4.2 us
  local copies, waits for them, and re-layouts: 38 us -> 7.18 us
  matrix products: 26.5 us -> 0 us
  blocking collectives: 23.6 us -> 0 us
    psum x1 -> x0, waiting for transfers between devices: 92.6 us -> none  [body(): lap_sum = lax.psum(scaled, 'gz')]
    all_gather x1 -> x0, waiting for transfers between devices: 63 us -> none  [entering_2(): gathered = jax.tree.map(lambda a: lax.all_gather(a, axis), part)]
    pallas_call x0 -> x1, Pallas kernels: none -> 49.8 us  [body(): pl.pallas_call(functools.partial(kernel, loop_size, layers, rows), out_sh...]
    dot_general x4 -> x0, matrix products: 26.5 us -> none  [the longest x1 13.8 us: build_upward(): jnp.einsum('kij,kjb->kib', decay_table, box_terms, precision=lax.Precisio...]
    all_gather x1 -> x0, blocking collectives: 23.6 us -> none  [entering_2(): gathered = jax.tree.map(lambda a: lax.all_gather(a, axis), part)]
    scatter-add x1 -> x0, local copies, waits for them, and re-layouts: 18.9 us -> none  [build_upward(): upward = upward.at[:, 0, :].add(-factor * before_term)]
    concatenate x7 -> x3, other arithmetic: 17.3 us -> 2.49 us  [the longest x1 1.48 us: body(): jnp.concatenate([jnp.pad(x2l, spare), jnp.pad(swapped, spare)], axis=0)]
    another operation x2 -> x0, other arithmetic: 14 us -> none
  transfers between devices with their start and end apart: 5 -> 0, of which waited for: 2 -> 0; matrix products, arithmetic and copies ran while one was open for 2% -> 0% of each run, Pallas kernels for 0% -> 0%
where the time goes in v1:
time: 61.6 us; the launch traced here: 61.3 us
  Pallas kernels  49.8 us (81%)
  local copies, waits for them, and re-layouts  7.18 us (12%)
  other arithmetic  4.2 us (7%)
    pallas_call x1, Pallas kernels, body(): pl.pallas_call(functools.partial(kernel, loop_size, layers, rows), out_sh...  49.8 us
    unnamed x13, local copies, waits for them, and re-layouts  3.88 us
    concatenate x1, other arithmetic, body(): jnp.concatenate([jnp.pad(x2l, spare), jnp.pad(swapped, spare)], axis=0)  1.48 us

profile of v1, /device:TPU:0, one launch (start us, length us, event | category | flops | bytes accessed | tf_op | source)
XLA Modules:
  0.0 61.3 jit_solution(9504022865967125212)
XLA Ops:
  0.0 0.7 %convert_element_type.20 = f32[6,2]{0,1:T(2,128)S(1)} convert(s32[6,2]{0,1:T(2,128)} %param.15) | non-fusion elementwise | flops 12 | bytes 96 | tf_op jit(solution)/shard_map/convert_element_type | solution.py:270
  0.7 0.9 %fusion.9 = (f32[6,648]{1,0:T(8,128)S(1)}, f32[6,648]{1,0:T(8,128)S(1)}, f32[6,648]{1,0:T(8,128)S(1)}) fusion(f32[648]{0:T(1024)} %param.14, f32[6]{0:T(128)S(1)} %get-tuple-element.11, f32[648]{0:T(1024)} %param.13, f32[6]{0:T(128)S(1)} %get-tuple-element.10), kind=kLoop, calls=%fused_computation.15 | loop fusion | flops 15552 | bytes 51888 | tf_op jit(solution)/shard_map/cos | solution.py:272
  1.6 0.7 %fusion.6.cs_ref = f32[16,1296]{1,0:T(8,128)} fusion(f32[6,648]{1,0:T(8,128)S(1)} %get-tuple-element.8, f32[6,648]{1,0:T(8,128)S(1)} %get-tuple-element.9, f32[6,648]{1,0:T(8,128)S(1)} %get-tuple-element.7, f32[2,1296]{1,0:T(2,128)S(1)} %broadcast_in_dim.6), kind=kLoop, calls=%fused_computation.10 | loop fusion | flops 103680 | bytes 139968 | tf_op jit(solution)/shard_map/concatenate | solution.py:274
  2.3 1.7 %copy.9 = bf16[361,1296]{1,0:T(8,128)(2,1)S(1)} copy(bf16[361,1296]{0,1:T(8,128)(2,1)} %param.11) | data formatting | bytes 1871424 | tf_op args[3]
  4.0 0.2 fusion.11
  4.2 0.3 fusion.4
  4.5 0.0 copy-start.3
  4.6 0.0 copy-start
  4.6 1.5 %fusion.1.xs_ref = bf16[736,1296]{1,0:T(8,128)(2,1)} fusion(bf16[361,1296]{1,0:T(8,128)(2,1)S(1)} %copy.9, bf16[368,1296]{1,0:T(8,128)(2,1)S(1)} %fusion.4), kind=kLoop, calls=%fused_computation.2 | loop fusion | flops 5723136 | bytes 3797280 | tf_op jit(solution)/shard_map/concatenate | solution.py:269
  6.0 0.0 copy-done.3
  6.0 0.0 copy-done
  6.1 0.1 multiply_convert_fusion
  6.2 0.0 copy-start.1
  6.2 0.1 pad.33
  6.3 0.0 copy-start.2
  6.3 0.2 copy.13
  6.5 1.0 %pad.11.mp_ref = bf16[368,1024]{1,0:T(8,128)(2,1)} pad(bf16[361,1024]{1,0:T(8,128)(2,1)S(1)} %bitcast.11, bf16[]{:T(256)} %constant.1.clone.1), padding=0_7x0_0 | pad | bytes 1492994 | tf_op jit(solution)/shard_map/jit(_pad)/pad | solution.py:266
  7.4 0.0 copy-done.1
  7.4 0.1 concatenate.23
  7.5 1.1 %broadcast_in_dim.8.rate_ref = f32[1344,128]{1,0:T(8,128)} broadcast(f32[1344]{0:T(1024)S(1)} %concatenate.23), dimensions={0} | broadcast | bytes 693504 | tf_op jit(solution)/shard_map/broadcast_in_dim | solution.py:278
  8.6 0.0 copy-done.2
  8.6 0.7 %copy.12.off_ref = s32[6,2]{1,0:T(8,128)} copy(s32[6,2]{0,1:T(2,128)S(1)} %copy-done.2) | data formatting | bytes 96 | tf_op args[7]
  9.3 49.8 %shard_map.82 = bf16[368,1024]{1,0:T(8,128)(2,1)} custom-call(s32[6,2]{1,0:T(8,128)} %copy.12.off_ref, bf16[368,1024]{1,0:T(8,128)(2,1)} %pad.11.mp_ref, bf16[1296,361]{1,0:T(8,128)(2,1)} %m2x_ref.1, bf16[736,1296]{1,0:T(8,128)(2,1)} %fusion.1.xs_ref, f32[16,1296]{1,0:T(8,128)} %fusion.6.cs_ref, f32[1344,128]{1,0:T(8,128)} %broadcast_in_dim.8.rate_ref), custom_call_target="tpu_custom_call" | custom-call | flops 7665352704 | bytes 6291456 | tf_op jit(solution)/shard_map/pallas_call | solution.py:282
  59.1 1.3 %copy.14 = bf16[46,8,8,128]{3,2,1,0:T(8,128)(2,1)S(1)} copy(bf16[46,8,8,128]{3,1,2,0:T(8,128)(2,1)} %bitcast.14) | data formatting | bytes 1507328
  60.4 0.9 %slice.22 = bf16[361,8,128]{2,1,0:T(8,128)(2,1)} slice(bf16[368,8,128]{2,1,0:T(8,128)(2,1)S(1)} %bitcast.13), slice={[0:361], [0:8], [0:128]} | slice | bytes 1478656 | tf_op jit(solution)/shard_map/reshape | solution.py:318
  (4 shorter events, 0.0 us)
Async XLA Ops:
  4.5 1.5 %copy-start.3 = (s32[8,128]{1,0:T(8,128)S(1)}, s32[8,128]{1,0:T(8,128)}, u32[]{:S(2)}) copy-start(s32[8,128]{1,0:T(8,128)} %param.9) | copy-start | bytes 12292
  4.6 1.5 %copy-start = (bf16[361,8,128]{2,1,0:T(8,128)(2,1)S(1)}, bf16[361,8,128]{2,1,0:T(8,128)(2,1)}, u32[]{:S(2)}) copy-start(bf16[361,8,128]{2,1,0:T(8,128)(2,1)} %param.8) | copy-start | bytes 2217988
  6.2 1.2 %copy-start.1 = (f32[648]{0:T(1024)S(1)}, f32[648]{0:T(1024)}, u32[]{:S(2)}) copy-start(f32[648]{0:T(1024)} %param.12) | copy-start | bytes 7780
  6.3 2.3 %copy-start.2 = (s32[6,2]{0,1:T(2,128)S(1)}, s32[6,2]{0,1:T(2,128)}, u32[]{:S(2)}) copy-start(s32[6,2]{0,1:T(2,128)} %param.15) | copy-start | bytes 148

commit v2 on v1

v2 whole, which is shorter than its diff:
```python
import functools

import jax
import jax.numpy as jnp
from jax import lax
from jax.experimental import pallas as pl
from jax.experimental.pallas import tpu as pltpu
from jax.sharding import PartitionSpec as P

BY = 8
R = 2
NOFF = 6
GROUP = 4
BOXES = 128
MESH = pl.DeviceIdType.MESH
F32 = jnp.float32
BF16 = jnp.bfloat16


def up(value, step):
    return -(-value // step) * step


def kernel(
    loop_size, layers, rows,
    off_ref, moments_ref, counts_ref, m2x_ref, x2l_ref, decay_ref, wave_x_ref, wave_y_ref,
    out_ref,
    charged, poles, rates, phases, terms, outgo, top_out, top, below, ingroup, planes, entbuf,
    enter, wall, upward, total_z, perm, place, mixed, own, edge, edge_out, edge_in,
    top_s, top_r, a_s, a_r, b_s, b_r, c_s, c_r, e_s, e_r,
):
    slab = lax.axis_index("gz")
    half = lax.axis_index("xy")
    groups = loop_size // GROUP
    group, member = slab // GROUP, lax.rem(slab, GROUP)
    after = lax.rem(slab + 1, loop_size)
    before = lax.rem(slab + loop_size - 1, loop_size)
    coeffs = m2x_ref.shape[1]
    out_rows = poles.shape[0]
    parts = split_rows(rows)

    def mate(step):
        return lax.rem(member + step, GROUP)

    def mate_id(step):
        return group * GROUP + mate(step)

    def plane_id(step):
        return lax.rem(group + step, groups) * GROUP + member

    barrier = pltpu.get_barrier_semaphore()
    partners = [after, before]
    partners += [mate_id(step) for step in range(1, GROUP)]
    partners += [plane_id(step) for step in range(1, groups)]
    for partner in partners:
        pl.semaphore_signal(barrier, inc=1, device_id={"gz": partner}, device_id_type=MESH)
    pl.semaphore_signal(barrier, inc=1, device_id={"xy": 1 - half}, device_id_type=MESH)

    count = counts_ref[...].astype(F32)

    @pl.loop(0, coeffs // 8)
    def _(turn):
        part = moments_ref[pl.ds(turn * 8, 8)].astype(F32) * count[None]
        charged[pl.ds(pl.multiple_of(turn * 64, 64), 64), :] = part.reshape(64, BOXES)

    done = coeffs // 8 * 8
    part = moments_ref[done:coeffs].astype(F32) * count[None]
    charged[done * 8:coeffs * 8, :] = part.reshape((coeffs - done) * 8, BOXES)
    charged[coeffs * 8:, :] = jnp.zeros(((out_rows - coeffs) * 8, BOXES), F32)
    for z in range(layers):
        layer = charged[pl.ds(z, out_rows, stride=8), :].astype(BF16)
        poles[:, z * BOXES:(z + 1) * BOXES] = layer
        if z == layers - 1:
            top_out[...] = layer

    pl.semaphore_wait(barrier, len(partners) + 1)

    top_copy = pltpu.make_async_remote_copy(
        src_ref=top_out, dst_ref=top, send_sem=top_s, recv_sem=top_r,
        device_id={"gz": after}, device_id_type=MESH,
    )
    top_copy.start()

    decay_row = decay_ref[...]
    spare = rates.shape[0] - rows
    decay_row = jnp.concatenate([decay_row, decay_row, jnp.full((1, spare), 0.01, F32)], axis=1)
    for turn in range(rates.shape[0] // BOXES):
        at = slice(turn * BOXES, (turn + 1) * BOXES)
        rates[at, :] = jnp.transpose(jnp.broadcast_to(decay_row[:, at], (BOXES, BOXES)))

    def strip(base, turn):
        return pl.ds(pl.multiple_of(base + turn * 16, 16), 16)

    def lot(base, index, size):
        return pl.ds(pl.multiple_of(base + index * size, 16), size)

    a_copies = []
    for index, (base, size, real, inner, quarter) in enumerate(parts):
        terms[base:base + real, :] = jnp.dot(
            m2x_ref[base:base + real, :], poles[0:coeffs, :], preferred_element_type=F32)

        @pl.loop(0, real // 16)
        def _(turn):
            at = strip(base, turn)
            factor = jnp.exp(-rates[at, :])
            square = factor * factor
            weight = jnp.sqrt(1.0 - square)
            box = [weight * terms[at, z * BOXES:(z + 1) * BOXES] for z in range(layers)]
            total = box[0]
            for z in range(1, layers):
                total = factor * total + box[z]
            outgo[at, :] = total.astype(BF16)
            state = jnp.zeros_like(factor)
            for z in range(2, layers):
                state = factor * state + square * box[z - 2]
                terms[at, z * BOXES:(z + 1) * BOXES] = state

        if size > real:
            outgo[base + real:base + size, :] = jnp.zeros((size - real, BOXES), BF16)
        copies = []
        for step in range(1, GROUP):
            sem = index * GROUP + step
            copy = pltpu.make_async_remote_copy(
                src_ref=outgo.at[lot(base, mate(step), quarter), :],
                dst_ref=ingroup.at[step, pl.ds(inner, quarter), :],
                send_sem=a_s.at[sem], recv_sem=a_r.at[sem],
                device_id={"gz": mate_id(step)}, device_id_type=MESH,
            )
            copy.start()
            copies.append(copy)
        a_copies.append(copies)
        ingroup[0, inner:inner + quarter, :] = outgo[lot(base, member, quarter), :]

    row = lax.broadcasted_iota(jnp.int32, (8, rows), 0)
    side = lax.broadcasted_iota(jnp.int32, (8, rows), 1)
    step_x = jnp.zeros((8, rows), F32)
    step_y = jnp.zeros((8, rows), F32)
    for entry in range(NOFF):
        step_x = jnp.where(row == entry, off_ref[entry, 0].astype(F32), step_x)
        step_y = jnp.where(row == entry, off_ref[entry, 1].astype(F32), step_y)
    wave_x = jnp.concatenate([wave_x_ref[...], wave_x_ref[...]], axis=1)
    wave_y = jnp.concatenate([wave_y_ref[...], wave_y_ref[...]], axis=1)
    angle = wave_x * step_x + wave_y * step_y
    sine = jnp.sin(angle)
    phases[0:8, :] = jnp.cos(angle)
    phases[8:16, :] = jnp.where(side < rows // 2, sine, -sine)

    def phase_maps(x2l, place_of):
        real = x2l.astype(F32)
        swap = jnp.concatenate([real[:, rows // 2:], real[:, :rows // 2]], axis=1)
        for entry in range(NOFF):
            mix = real * phases[entry:entry + 1, :] + swap * phases[8 + entry:9 + entry, :]
            if mix.shape[0] < 16:
                mix = jnp.concatenate([mix, jnp.zeros((16 - mix.shape[0], rows), F32)], axis=0)
            wall[place_of(entry * out_rows), :] = mix.astype(BF16)

    def some_maps(low, high):
        @pl.loop(low, high)
        def _(turn):
            phase_maps(x2l_ref[strip(0, turn), :], lambda base: strip(base, turn))

    def send_planes(index):
        base, size, real, inner, quarter = parts[index]
        for copy in a_copies[index]:
            copy.wait_recv()
        decay = jnp.exp(-rates[lot(base, member, quarter), :] * layers)
        total = source(0, index)
        for other in range(1, GROUP):
            total = decay * total + source(other, index)
        planes[0, inner:inner + quarter, :] = total.astype(BF16)
        copies = []
        for step in range(1, groups):
            sem = index * groups + step
            copy = pltpu.make_async_remote_copy(
                src_ref=planes.at[0, pl.ds(inner, quarter), :],
                dst_ref=planes.at[step, pl.ds(inner, quarter), :],
                send_sem=b_s.at[sem], recv_sem=b_r.at[sem],
                device_id={"gz": plane_id(step)}, device_id_type=MESH,
            )
            copy.start()
            copies.append(copy)
        return copies

    def source(other, index):
        base, size, real, inner, quarter = parts[index]
        return ingroup[lax.rem(member - other + GROUP, GROUP), inner:inner + quarter, :].astype(F32)

    def send_entering(index):
        base, size, real, inner, quarter = parts[index]
        for copy in b_copies[index]:
            copy.wait_recv()
        at = slice(inner, inner + quarter)
        rate = rates[lot(base, member, quarter), :]
        decay = jnp.exp(-rate * layers)
        plane_decay = jnp.exp(-rate * (layers * GROUP))
        total = planes[0, at, :].astype(F32)
        for step in range(groups - 1, 0, -1):
            total = plane_decay * total + planes[step, at, :].astype(F32)
        state = total / (1.0 - jnp.exp(-rate * (layers * loop_size)))
        entbuf[0, at, :] = state.astype(BF16)
        for other in range(1, GROUP):
            state = decay * state + source(other - 1, index)
            entbuf[other, at, :] = state.astype(BF16)
        copies = []
        for step in range(1, GROUP):
            sem = index * GROUP + step
            copy = pltpu.make_async_remote_copy(
                src_ref=entbuf.at[mate(step), pl.ds(inner, quarter), :],
                dst_ref=enter.at[lot(base, member, quarter), :],
                send_sem=c_s.at[sem], recv_sem=c_r.at[sem],
                device_id={"gz": mate_id(step)}, device_id_type=MESH,
            )
            copy.start()
            copies.append(copy)
        enter[lot(base, member, quarter), :] = entbuf[member, at, :]
        return copies

    def raise_part(index):
        base, size, real, inner, quarter = parts[index]
        for step in range(1, GROUP):
            sem = index * GROUP + step
            sender = lax.rem(member - step + GROUP, GROUP)
            pltpu.make_async_remote_copy(
                src_ref=entbuf.at[0, pl.ds(inner, quarter), :],
                dst_ref=enter.at[lot(base, sender, quarter), :],
                send_sem=c_s.at[sem], recv_sem=c_r.at[sem],
                device_id={"gz": mate_id(step)}, device_id_type=MESH,
            ).wait_recv()

        @pl.loop(0, real // 16)
        def _(turn):
            at = strip(base, turn)
            factor = jnp.exp(-rates[at, :])
            weight = jnp.sqrt(1.0 - factor * factor)
            state = factor * enter[at, :].astype(F32)
            upward[at, 0:BOXES] = (state - factor * (weight * below[at, :])).astype(BF16)
            state = factor * state
            upward[at, BOXES:2 * BOXES] = state.astype(BF16)
            for z in range(2, layers):
                state = factor * state
                upward[at, z * BOXES:(z + 1) * BOXES] = (
                    state + terms[at, z * BOXES:(z + 1) * BOXES]).astype(BF16)

    def map_part(index, entry, pair):
        base, size, real, inner, quarter = parts[index]
        two = pl.multiple_of(pair * 2 * BOXES, 2 * BOXES)
        return jnp.dot(
            wall[pl.ds(pl.multiple_of(entry * 2 * out_rows, 16), 2 * out_rows), base:base + real],
            upward[base:base + real, pl.ds(two, 2 * BOXES)],
            preferred_element_type=F32)

    def add_part(index):
        @pl.loop(0, layers // 2)
        def _(pair):
            @pl.loop(0, NOFF // 2)
            def _(entry):
                if index == 0:
                    total_z[pair, entry] = map_part(index, entry, pair)
                else:
                    total_z[pair, entry] += map_part(index, entry, pair)

    full = coeffs // 16
    b_copies = [send_planes(0)]
    some_maps(0, full // 2)
    b_copies.append(send_planes(1))
    some_maps(full // 2, full)
    phase_maps(x2l_ref[full * 16:coeffs, :], lambda base: pl.ds(base + full * 16, 16))
    b_copies.append(send_planes(2))

    lane = lax.broadcasted_iota(jnp.int32, (BOXES, 2 * BOXES), 0)
    column = lax.broadcasted_iota(jnp.int32, (BOXES, 2 * BOXES), 1)
    width = BOXES // BY
    for entry in range(NOFF):
        moved_x = lane // BY + off_ref[entry, 0]
        moved_y = (lane + off_ref[entry, 1]) & (BY - 1)
        inside = moved_x * BY + moved_y
        low = (moved_x + R) * BY + moved_y + BOXES
        high = (moved_x - width + R) * BY + moved_y + BOXES
        stays = (moved_x >= 0) & (moved_x < width)
        outside = jnp.where(moved_x < 0, low, high)
        for slot in range(4):
            target = jnp.where(stays, inside, outside + slot * 2 * R * BY)
            perm[slot, entry * BOXES:(entry + 1) * BOXES, :] = jnp.where(
                column == target, 1.0, 0.0).astype(BF16)
    lane = lax.broadcasted_iota(jnp.int32, (BOXES, BOXES), 0)
    column = lax.broadcasted_iota(jnp.int32, (BOXES, BOXES), 1)
    for slot in range(4):
        inner = lane - slot * 2 * R * BY
        target = jnp.where(inner < R * BY, inner + BOXES - R * BY, inner - R * BY)
        hit = (inner >= 0) & (inner < 2 * R * BY) & (column == target)
        place[slot] = jnp.where(hit, 1.0, 0.0).astype(BF16)

    top_copy.wait_recv()
    below[...] = jnp.dot(m2x_ref[...], top[0:coeffs, :], preferred_element_type=F32)

    c_copies = [send_entering(0), send_entering(1)]
    raise_part(0)
    c_copies.append(send_entering(2))
    add_part(0)
    raise_part(1)
    add_part(1)
    raise_part(2)

    e_copies = []
    for pair in range(layers // 2):
        for entry in range(NOFF // 2):
            part = (total_z[pair, entry] + map_part(2, entry, pair)).astype(BF16)
            for which in range(2):
                at = slice((entry * 2 + which) * BOXES, (entry * 2 + which + 1) * BOXES)
                mine = part[which * out_rows:(which + 1) * out_rows]
                mixed[0, :, at] = mine[:, :BOXES]
                mixed[1, :, at] = mine[:, BOXES:]

        for inner in range(2):
            z = pair * 2 + inner
            placed = jnp.dot(mixed[inner], perm[z % 4], preferred_element_type=F32)
            own[:, z * BOXES:(z + 1) * BOXES] = placed[:, :BOXES]
            if z % 4 == 0:
                edge[...] = placed[:, BOXES:]
            else:
                edge[...] += placed[:, BOXES:]
        if pair % 2 == 1:
            side = pair // 2
            edge_out[side] = edge[...].astype(BF16)
            copy = pltpu.make_async_remote_copy(
                src_ref=edge_out.at[side], dst_ref=edge_in.at[side],
                send_sem=e_s.at[side], recv_sem=e_r.at[side],
                device_id={"xy": 1 - half}, device_id_type=MESH,
            )
            copy.start()
            e_copies.append(copy)

    for side, copy in enumerate(e_copies):
        copy.wait_recv()
        for slot in range(4):
            at = slice((side * 4 + slot) * BOXES, (side * 4 + slot + 1) * BOXES)
            out_ref[:, at] = (
                own[:, at] + jnp.dot(edge_in[side], place[slot], preferred_element_type=F32)
            ).astype(BF16)[:coeffs]

    sent = [top_copy] + e_copies
    for copies in a_copies + b_copies + c_copies:
        sent += copies
    for copy in sent:
        copy.wait_send()


def split_rows(rows):
    first = up(rows // 3, BOXES)
    parts, base, inner = [], 0, 0
    while base < rows:
        real = min(first, rows - base)
        size = up(real, 16 * GROUP)
        parts.append((base, size, real, inner, size // GROUP))
        base, inner = base + real, inner + size // GROUP
    return parts


def body(moments, counts, m2x, x2l, decay_rate, wave_x, wave_y, offsets):
    coeffs, layers, plane_size = moments.shape
    rows = m2x.shape[0]
    loop_size = lax.axis_size("gz")
    groups = loop_size // GROUP
    parts = split_rows(rows)
    padded = parts[-1][0] + parts[-1][1]
    quarter = parts[-1][3] + parts[-1][4]
    count = len(parts)
    in_rows = up(coeffs, 16)
    lanes = layers * plane_size

    vmem = pl.BlockSpec(memory_space=pltpu.VMEM)
    dma = pltpu.SemaphoreType.DMA
    out = pl.pallas_call(
        functools.partial(kernel, loop_size, layers, rows),
        out_shape=jax.ShapeDtypeStruct((coeffs, lanes), BF16),
        in_specs=[pl.BlockSpec(memory_space=pltpu.SMEM)] + [vmem] * 7,
        out_specs=vmem,
        scratch_shapes=[
            pltpu.VMEM((in_rows * 8, BOXES), F32),
            pltpu.VMEM((in_rows, lanes), BF16),
            pltpu.VMEM((up(padded, BOXES), BOXES), F32),
            pltpu.VMEM((16, rows), F32),
            pltpu.VMEM((rows, lanes), F32),
            pltpu.VMEM((padded, BOXES), BF16),
            pltpu.VMEM((in_rows, BOXES), BF16),
            pltpu.VMEM((in_rows, BOXES), BF16),
            pltpu.VMEM((rows, BOXES), F32),
            pltpu.VMEM((GROUP, quarter, BOXES), BF16),
            pltpu.VMEM((groups, quarter, BOXES), BF16),
            pltpu.VMEM((GROUP, quarter, BOXES), BF16),
            pltpu.VMEM((padded, BOXES), BF16),
            pltpu.VMEM((NOFF * in_rows, rows), BF16),
            pltpu.VMEM((rows, lanes), BF16),
            pltpu.VMEM((layers // 2, NOFF // 2, 2 * in_rows, 2 * BOXES), F32),
            pltpu.VMEM((4, NOFF * BOXES, 2 * BOXES), BF16),
            pltpu.VMEM((4, BOXES, BOXES), BF16),
            pltpu.VMEM((2, in_rows, NOFF * BOXES), BF16),
            pltpu.VMEM((in_rows, lanes), F32),
            pltpu.VMEM((in_rows, BOXES), F32),
            pltpu.VMEM((2, in_rows, BOXES), BF16),
            pltpu.VMEM((2, in_rows, BOXES), BF16),
            dma, dma,
            dma((count * GROUP,)), dma((count * GROUP,)),
            dma((count * groups,)), dma((count * groups,)),
            dma((count * GROUP,)), dma((count * GROUP,)),
            dma((2,)), dma((2,)),
        ],
        compiler_params=pltpu.CompilerParams(
            collective_id=0, has_side_effects=True, vmem_limit_bytes=58 * 2**20
        ),
        cost_estimate=pl.CostEstimate(
            flops=16 * rows * coeffs * lanes, bytes_accessed=6 * 2**20, transcendentals=0
        ),
    )(offsets, moments, counts, m2x, x2l, decay_rate[None], wave_x[None], wave_y[None])
    return out.reshape(coeffs, layers, plane_size)


def solution(mesh):
    in_specs = (P(None, "gz", "xy"), P("gz", "xy"), P(), P(), P(), P(), P(), P())
    out_specs = P(None, "gz", "xy")
    return jax.shard_map(body, mesh=mesh, in_specs=in_specs, out_specs=out_specs, check_vma=False)
```

time: 61.6 us -> 50.9 us (0.83)
  Pallas kernels: 49.8 us -> 42.7 us
  other arithmetic: 4.2 us -> 0 us
  local copies, waits for them, and re-layouts: 7.18 us -> 7.93 us
    pallas_call x1, Pallas kernels: 49.8 us -> 42.7 us  [body(): pl.pallas_call(functools.partial(kernel, loop_size, layers, rows), out_sh...]
    concatenate x3 -> x0, other arithmetic: 2.49 us -> none  [the longest x1 1.48 us: body(): jnp.concatenate([jnp.pad(x2l, spare), jnp.pad(swapped, spare)], axis=0)]
    broadcast_in_dim x3, local copies, waits for them, and re-layouts: 1.1 us -> 2.46 us  [the longest x1 1.29 us: body(): decay_rate[None]]
    pad x1 -> x0, local copies, waits for them, and re-layouts: 0.95 us -> none  [body(): jnp.pad(multipole.reshape(coeffs, lanes), ((0, in_rows - coeffs), (0, 0)))]
    cos x1 -> x0, other arithmetic: 0.87 us -> none  [body(): cosine, sine = (jnp.cos(angle), jnp.sin(angle))]
    convert_element_type x3 -> x0, other arithmetic: 0.83 us -> none  [the longest x1 0.68 us: body(): steps = offsets.astype(F32)]
    unnamed x13 -> x9, local copies, waits for them, and re-layouts: 3.88 us -> 4.55 us
where the time goes in v2:
time: 50.9 us; the launch traced here: 50.6 us
  Pallas kernels  42.7 us (84%)
  local copies, waits for them, and re-layouts  7.93 us (16%)
    pallas_call x1, Pallas kernels, body(): pl.pallas_call(functools.partial(kernel, loop_size, layers, rows), out_sh...  42.7 us
    unnamed x9, local copies, waits for them, and re-layouts  4.55 us
    broadcast_in_dim x1, local copies, waits for them, and re-layouts, body(): decay_rate[None]  1.29 us

profile of v2, /device:TPU:0, one launch (start us, length us, event | category | flops | bytes accessed | tf_op | source)
XLA Modules:
  0.0 50.6 jit_solution(7138422536044679849)
XLA Ops:
  0.0 0.0 copy-start
  0.0 1.3 %broadcast_in_dim.9.decay_ref = f32[1,648]{1,0:T(1,128)} reshape(f32[648]{0:T(1024)} %param.12) | data formatting | bytes 5184 | tf_op jit(solution)/shard_map/broadcast_in_dim | solution.py:414
  1.3 0.0 copy-done
  1.3 0.0 copy-start.1
  1.3 0.6 %broadcast_in_dim.10.wave_x_ref = f32[1,648]{1,0:T(1,128)} reshape(f32[648]{0:T(1024)S(1)} %copy-done) | data formatting | bytes 5184 | tf_op jit(solution)/shard_map/broadcast_in_dim | solution.py:414
  1.9 0.1 copy-done.1
  2.0 0.0 copy-start.2
  2.0 0.6 %broadcast_in_dim.11.wave_y_ref = f32[1,648]{1,0:T(1,128)} reshape(f32[648]{0:T(1024)S(1)} %copy-done.1) | data formatting | bytes 5184 | tf_op jit(solution)/shard_map/broadcast_in_dim | solution.py:414
  2.6 0.1 copy-done.2
  2.7 0.7 %copy.9.off_ref = s32[6,2]{1,0:T(8,128)} copy(s32[6,2]{0,1:T(2,128)S(1)} %copy-done.2) | data formatting | bytes 96 | tf_op args[7]
  3.3 2.4 %copy.10.x2l_ref = bf16[361,1296]{1,0:T(8,128)(2,1)} copy(bf16[361,1296]{0,1:T(8,128)(2,1)} %param.11) | data formatting | bytes 1871424 | tf_op args[3]
  5.7 42.7 %shard_map.82 = bf16[361,1024]{1,0:T(8,128)(2,1)} custom-call(s32[6,2]{1,0:T(8,128)} %copy.9.off_ref, bf16[361,8,128]{2,1,0:T(8,128)(2,1)} %moments_ref.1, s32[8,128]{1,0:T(8,128)} %counts_ref.1, bf16[1296,361]{1,0:T(8,128)(2,1)} %m2x_ref.1, bf16[361,1296]{1,0:T(8,128)(2,1)} %copy.10.x2l_ref, f32[1,648]{1,0:T(1,128)} %broadcast_in_dim.9.decay_ref, ...), custom_call_target="tpu_custom_call" | custom-call | flops 7665352704 | bytes 6291456 | tf_op jit(solution)/shard_map/pallas_call | solution.py:373
  48.4 1.3 %copy.11 = bf16[46,8,8,128]{3,2,1,0:T(8,128)(2,1)S(1)} copy(bf16[46,8,8,128]{3,1,2,0:T(8,128)(2,1)} %bitcast.4) | data formatting | bytes 1507328
  49.7 0.9 %slice = bf16[361,8,128]{2,1,0:T(8,128)(2,1)} slice(bf16[368,8,128]{2,1,0:T(8,128)(2,1)S(1)} %bitcast.3), slice={[0:361], [0:8], [0:128]} | slice | bytes 1478656 | tf_op jit(solution)/shard_map/reshape | solution.py:415
Async XLA Ops:
  0.0 1.3 %copy-start = (f32[648]{0:T(1024)S(1)}, f32[648]{0:T(1024)}, u32[]{:S(2)}) copy-start(f32[648]{0:T(1024)} %param.13) | copy-start | bytes 7780
  1.3 0.7 %copy-start.1 = (f32[648]{0:T(1024)S(1)}, f32[648]{0:T(1024)}, u32[]{:S(2)}) copy-start(f32[648]{0:T(1024)} %param.14) | copy-start | bytes 7780
  2.0 0.7 %copy-start.2 = (s32[6,2]{0,1:T(2,128)S(1)}, s32[6,2]{0,1:T(2,128)}, u32[]{:S(2)}) copy-start(s32[6,2]{0,1:T(2,128)} %param.15) | copy-start | bytes 148

commit v3 on v2

--- a/solution.py
+++ b/solution.py
@@ -25,7 +25,7 @@
     loop_size, layers, rows,
     off_ref, moments_ref, counts_ref, m2x_ref, x2l_ref, decay_ref, wave_x_ref, wave_y_ref,
     out_ref,
-    charged, poles, rates, phases, terms, outgo, top_out, top, below, ingroup, planes, entbuf,
+    charged, poles, rates, factors, weights, spread, phases, terms, outgo, top_out, top, below, ingroup, planes, entbuf,
     enter, wall, upward, total_z, perm, place, mixed, own, edge, edge_out, edge_in,
     top_s, top_r, a_s, a_r, b_s, b_r, c_s, c_r, e_s, e_r,
 ):
@@ -73,6 +73,18 @@
         if z == layers - 1:
             top_out[...] = layer
 
+    long_rows = rates.shape[0]
+    spare = long_rows - rows
+    decay_row = decay_ref[...].reshape(1, rows // 2)
+    decay_row = jnp.concatenate([decay_row, decay_row, jnp.full((1, spare), 0.01, F32)], axis=1)
+    for turn in range(long_rows // BOXES):
+        at = slice(turn * BOXES, (turn + 1) * BOXES)
+        rate = jnp.transpose(jnp.broadcast_to(decay_row[:, at], (BOXES, BOXES)))
+        factor = jnp.exp(-rate)
+        rates[at, :] = rate
+        factors[at, :] = factor
+        weights[at, :] = jnp.sqrt(1.0 - factor * factor)
+
     pl.semaphore_wait(barrier, len(partners) + 1)
 
     top_copy = pltpu.make_async_remote_copy(
@@ -81,15 +93,13 @@
     )
     top_copy.start()
 
-    decay_row = decay_ref[...]
-    spare = rates.shape[0] - rows
-    decay_row = jnp.concatenate([decay_row, decay_row, jnp.full((1, spare), 0.01, F32)], axis=1)
-    for turn in range(rates.shape[0] // BOXES):
-        at = slice(turn * BOXES, (turn + 1) * BOXES)
-        rates[at, :] = jnp.transpose(jnp.broadcast_to(decay_row[:, at], (BOXES, BOXES)))
-
-    def strip(base, turn):
-        return pl.ds(pl.multiple_of(base + turn * 16, 16), 16)
+    def strips(base, real, work):
+        @pl.loop(0, real // 32)
+        def _(turn):
+            work(pl.ds(pl.multiple_of(base + turn * 32, 32), 32))
+
+        if real % 32:
+            work(pl.ds(base + real // 32 * 32, real % 32))
 
     def lot(base, index, size):
         return pl.ds(pl.multiple_of(base + index * size, 16), size)
@@ -99,22 +109,20 @@
         terms[base:base + real, :] = jnp.dot(
             m2x_ref[base:base + real, :], poles[0:coeffs, :], preferred_element_type=F32)
 
-        @pl.loop(0, real // 16)
-        def _(turn):
-            at = strip(base, turn)
-            factor = jnp.exp(-rates[at, :])
+        def fold(at):
+            factor, weight = factors[at, :], weights[at, :]
             square = factor * factor
-            weight = jnp.sqrt(1.0 - square)
-            box = [weight * terms[at, z * BOXES:(z + 1) * BOXES] for z in range(layers)]
-            total = box[0]
-            for z in range(1, layers):
-                total = factor * total + box[z]
+            older = old = None
+            for z in range(layers):
+                box = weight * terms[at, z * BOXES:(z + 1) * BOXES]
+                total = box if z == 0 else factor * total + box
+                if z >= 2:
+                    state = square * older if z == 2 else factor * state + square * older
+                    terms[at, z * BOXES:(z + 1) * BOXES] = state
+                older, old = old, box
             outgo[at, :] = total.astype(BF16)
-            state = jnp.zeros_like(factor)
-            for z in range(2, layers):
-                state = factor * state + square * box[z - 2]
-                terms[at, z * BOXES:(z + 1) * BOXES] = state
-
+
+        strips(base, real, fold)
         if size > real:
             outgo[base + real:base + size, :] = jnp.zeros((size - real, BOXES), BF16)
         copies = []
@@ -131,33 +139,40 @@
         a_copies.append(copies)
         ingroup[0, inner:inner + quarter, :] = outgo[lot(base, member, quarter), :]
 
-    row = lax.broadcasted_iota(jnp.int32, (8, rows), 0)
-    side = lax.broadcasted_iota(jnp.int32, (8, rows), 1)
-    step_x = jnp.zeros((8, rows), F32)
-    step_y = jnp.zeros((8, rows), F32)
+    row = lax.broadcasted_iota(jnp.int32, (8, long_rows), 0)
+    side = lax.broadcasted_iota(jnp.int32, (8, long_rows), 1)
+    step_x = jnp.zeros((8, long_rows), F32)
+    step_y = jnp.zeros((8, long_rows), F32)
     for entry in range(NOFF):
-        step_x = jnp.where(row == entry, off_ref[entry, 0].astype(F32), step_x)
-        step_y = jnp.where(row == entry, off_ref[entry, 1].astype(F32), step_y)
-    wave_x = jnp.concatenate([wave_x_ref[...], wave_x_ref[...]], axis=1)
-    wave_y = jnp.concatenate([wave_y_ref[...], wave_y_ref[...]], axis=1)
+        step_x = jnp.where(row == entry, off_ref[0, entry].astype(F32), step_x)
+        step_y = jnp.where(row == entry, off_ref[1, entry].astype(F32), step_y)
+    gap = jnp.zeros((1, spare), F32)
+    wave_x = wave_x_ref[...].reshape(1, rows // 2)
+    wave_y = wave_y_ref[...].reshape(1, rows // 2)
+    wave_x = jnp.concatenate([wave_x, wave_x, gap], axis=1)
+    wave_y = jnp.concatenate([wave_y, wave_y, gap], axis=1)
     angle = wave_x * step_x + wave_y * step_y
     sine = jnp.sin(angle)
     phases[0:8, :] = jnp.cos(angle)
     phases[8:16, :] = jnp.where(side < rows // 2, sine, -sine)
-
-    def phase_maps(x2l, place_of):
-        real = x2l.astype(F32)
-        swap = jnp.concatenate([real[:, rows // 2:], real[:, :rows // 2]], axis=1)
-        for entry in range(NOFF):
-            mix = real * phases[entry:entry + 1, :] + swap * phases[8 + entry:9 + entry, :]
-            if mix.shape[0] < 16:
-                mix = jnp.concatenate([mix, jnp.zeros((16 - mix.shape[0], rows), F32)], axis=0)
-            wall[place_of(entry * out_rows), :] = mix.astype(BF16)
+    spread[:, up(coeffs, BOXES) - BOXES:] = jnp.zeros((long_rows, BOXES), F32)
+    spread[rows:, :] = jnp.zeros((spare, up(coeffs, BOXES)), F32)
+    spread[0:rows, 0:coeffs] = x2l_ref[...].astype(F32)
 
     def some_maps(low, high):
-        @pl.loop(low, high)
-        def _(turn):
-            phase_maps(x2l_ref[strip(0, turn), :], lambda base: strip(base, turn))
+        for turn in range(low, high):
+            at = slice(turn * BOXES, (turn + 1) * BOXES)
+            start = (turn * BOXES + rows // 2) % rows
+            if start + BOXES <= rows:
+                swap = spread[start:start + BOXES, :]
+            else:
+                swap = jnp.concatenate(
+                    [spread[start:rows, :], spread[0:start + BOXES - rows, :]], axis=0)
+            real = jnp.transpose(spread[at, :])[:out_rows]
+            swap = jnp.transpose(swap)[:out_rows]
+            for entry in range(NOFF):
+                mix = real * phases[entry:entry + 1, at] + swap * phases[8 + entry:9 + entry, at]
+                wall[entry * out_rows:(entry + 1) * out_rows, at] = mix.astype(BF16)
 
     def send_planes(index):
         base, size, real, inner, quarter = parts[index]
@@ -227,19 +242,18 @@
                 device_id={"gz": mate_id(step)}, device_id_type=MESH,
             ).wait_recv()
 
-        @pl.loop(0, real // 16)
-        def _(turn):
-            at = strip(base, turn)
-            factor = jnp.exp(-rates[at, :])
-            weight = jnp.sqrt(1.0 - factor * factor)
+        def lift(at):
+            factor = factors[at, :]
             state = factor * enter[at, :].astype(F32)
-            upward[at, 0:BOXES] = (state - factor * (weight * below[at, :])).astype(BF16)
+            upward[at, 0:BOXES] = (state - factor * (weights[at, :] * below[at, :])).astype(BF16)
             state = factor * state
             upward[at, BOXES:2 * BOXES] = state.astype(BF16)
             for z in range(2, layers):
                 state = factor * state
                 upward[at, z * BOXES:(z + 1) * BOXES] = (
                     state + terms[at, z * BOXES:(z + 1) * BOXES]).astype(BF16)
+
+        strips(base, real, lift)
 
     def map_part(index, entry, pair):
         base, size, real, inner, quarter = parts[index]
@@ -259,20 +273,19 @@
                 else:
                     total_z[pair, entry] += map_part(index, entry, pair)
 
-    full = coeffs // 16
+    turns = long_rows // BOXES
     b_copies = [send_planes(0)]
-    some_maps(0, full // 2)
+    some_maps(0, turns // 2)
     b_copies.append(send_planes(1))
-    some_maps(full // 2, full)
-    phase_maps(x2l_ref[full * 16:coeffs, :], lambda base: pl.ds(base + full * 16, 16))
+    some_maps(turns // 2, turns)
     b_copies.append(send_planes(2))
 
     lane = lax.broadcasted_iota(jnp.int32, (BOXES, 2 * BOXES), 0)
     column = lax.broadcasted_iota(jnp.int32, (BOXES, 2 * BOXES), 1)
     width = BOXES // BY
     for entry in range(NOFF):
-        moved_x = lane // BY + off_ref[entry, 0]
-        moved_y = (lane + off_ref[entry, 1]) & (BY - 1)
+        moved_x = lane // BY + off_ref[0, entry]
+        moved_y = (lane + off_ref[1, entry]) & (BY - 1)
         inside = moved_x * BY + moved_y
         low = (moved_x + R) * BY + moved_y + BOXES
         high = (moved_x - width + R) * BY + moved_y + BOXES
@@ -334,9 +347,16 @@
         copy.wait_recv()
         for slot in range(4):
             at = slice((side * 4 + slot) * BOXES, (side * 4 + slot + 1) * BOXES)
-            out_ref[:, at] = (
-                own[:, at] + jnp.dot(edge_in[side], place[slot], preferred_element_type=F32)
-            ).astype(BF16)[:coeffs]
+            charged[pl.ds(side * 4 + slot, out_rows, stride=8), :] = (
+                own[:, at] + jnp.dot(edge_in[side], place[slot], preferred_element_type=F32))
+
+    @pl.loop(0, coeffs // 8)
+    def _(turn):
+        part = charged[pl.ds(pl.multiple_of(turn * 64, 64), 64), :]
+        out_ref[pl.ds(turn * 8, 8)] = part.reshape(8, 8, BOXES).astype(BF16)
+
+    out_ref[done:coeffs] = charged[done * 8:coeffs * 8, :].reshape(
+        coeffs - done, 8, BOXES).astype(BF16)
 
     sent = [top_copy] + e_copies
     for copies in a_copies + b_copies + c_copies:
@@ -348,8 +368,8 @@
 def split_rows(rows):
     first = up(rows // 3, BOXES)
     parts, base, inner = [], 0, 0
-    while base < rows:
-        real = min(first, rows - base)
+    for wanted in (first, first + BOXES, rows):
+        real = min(wanted, rows - base)
         size = up(real, 16 * GROUP)
         parts.append((base, size, real, inner, size // GROUP))
         base, inner = base + real, inner + size // GROUP
@@ -366,20 +386,24 @@
     quarter = parts[-1][3] + parts[-1][4]
     count = len(parts)
     in_rows = up(coeffs, 16)
+    long_rows = up(padded, BOXES)
     lanes = layers * plane_size
 
     vmem = pl.BlockSpec(memory_space=pltpu.VMEM)
     dma = pltpu.SemaphoreType.DMA
-    out = pl.pallas_call(
+    return pl.pallas_call(
         functools.partial(kernel, loop_size, layers, rows),
-        out_shape=jax.ShapeDtypeStruct((coeffs, lanes), BF16),
+        out_shape=jax.ShapeDtypeStruct(moments.shape, BF16),
         in_specs=[pl.BlockSpec(memory_space=pltpu.SMEM)] + [vmem] * 7,
         out_specs=vmem,
         scratch_shapes=[
             pltpu.VMEM((in_rows * 8, BOXES), F32),
             pltpu.VMEM((in_rows, lanes), BF16),
-            pltpu.VMEM((up(padded, BOXES), BOXES), F32),
-            pltpu.VMEM((16, rows), F32),
+            pltpu.VMEM((long_rows, BOXES), F32),
+            pltpu.VMEM((long_rows, BOXES), F32),
+            pltpu.VMEM((long_rows, BOXES), F32),
+            pltpu.VMEM((long_rows, up(coeffs, BOXES)), F32),
+            pltpu.VMEM((16, long_rows), F32),
             pltpu.VMEM((rows, lanes), F32),
             pltpu.VMEM((padded, BOXES), BF16),
             pltpu.VMEM((in_rows, BOXES), BF16),
@@ -389,7 +413,7 @@
             pltpu.VMEM((groups, quarter, BOXES), BF16),
             pltpu.VMEM((GROUP, quarter, BOXES), BF16),
             pltpu.VMEM((padded, BOXES), BF16),
-            pltpu.VMEM((NOFF * in_rows, rows), BF16),
+            pltpu.VMEM((NOFF * in_rows, long_rows), BF16),
             pltpu.VMEM((rows, lanes), BF16),
             pltpu.VMEM((layers // 2, NOFF // 2, 2 * in_rows, 2 * BOXES), F32),
             pltpu.VMEM((4, NOFF * BOXES, 2 * BOXES), BF16),
@@ -411,8 +435,7 @@
         cost_estimate=pl.CostEstimate(
             flops=16 * rows * coeffs * lanes, bytes_accessed=6 * 2**20, transcendentals=0
         ),
-    )(offsets, moments, counts, m2x, x2l, decay_rate[None], wave_x[None], wave_y[None])
-    return out.reshape(coeffs, layers, plane_size)
+    )(offsets.T, moments, counts, m2x, x2l.T, decay_rate, wave_x, wave_y)
 
 
 def solution(mesh):

time: 50.9 us -> 43.9 us (0.86)
  local copies, waits for them, and re-layouts: 7.93 us -> 2.03 us
  Pallas kernels: 42.7 us -> 41.7 us
    unnamed x9 -> x1, local copies, waits for them, and re-layouts: 4.55 us -> 2.03 us
    broadcast_in_dim x3 -> x0, local copies, waits for them, and re-layouts: 2.46 us -> none  [the longest x1 1.29 us: body(): decay_rate[None]]
    pallas_call x1, Pallas kernels: 42.7 us -> 41.7 us  [body(): pl.pallas_call(functools.partial(kernel, loop_size, layers, rows), out_sh...]
    reshape x1 -> x0, local copies, waits for them, and re-layouts: 0.92 us -> none  [body(): return out.reshape(coeffs, layers, plane_size)]
where the time goes in v3:
time: 43.9 us; the launch traced here: 43.7 us
  Pallas kernels  41.7 us (95%)
  local copies, waits for them, and re-layouts  2.03 us (5%)
    pallas_call x1, Pallas kernels, body(): pl.pallas_call(functools.partial(kernel, loop_size, layers, rows), out_sh...  41.7 us
    unnamed x1, local copies, waits for them, and re-layouts  2.03 us

profile of v3, /device:TPU:0, one launch (start us, length us, event | category | flops | bytes accessed | tf_op | source)
XLA Modules:
  0.0 43.7 jit_solution(10005760287872972386)
XLA Ops:
  0.0 41.7 %shard_map.82 = bf16[361,8,128]{2,1,0:T(8,128)(2,1)} custom-call(s32[2,6]{1,0:T(2,128)} %bitcast.3, bf16[361,8,128]{2,1,0:T(8,128)(2,1)} %moments_ref.1, s32[8,128]{1,0:T(8,128)} %counts_ref.1, bf16[1296,361]{1,0:T(8,128)(2,1)} %m2x_ref.1, bf16[1296,361]{1,0:T(8,128)(2,1)} %bitcast.2, f32[648]{0:T(1024)} %decay_ref.1, f32[648]{0:T(1024)} %wave_x_ref.1, ...), custom_call_target="tpu_custom_call" | custom-call | flops 7665352704 | bytes 6291456 | tf_op jit(solution)/shard_map/pallas_call | solution.py:394
  41.7 2.0 %copy.10 = bf16[361,8,128]{2,1,0:T(8,128)(2,1)} copy(bf16[361,8,128]{2,1,0:T(8,128)(2,1)} %shard_map.82) | data formatting | bytes 1478656

commit v4 on v3

--- a/solution.py
+++ b/solution.py
@@ -279,6 +279,7 @@
     b_copies.append(send_planes(1))
     some_maps(turns // 2, turns)
     b_copies.append(send_planes(2))
+    c_copies = [send_entering(0)]
 
     lane = lax.broadcasted_iota(jnp.int32, (BOXES, 2 * BOXES), 0)
     column = lax.broadcasted_iota(jnp.int32, (BOXES, 2 * BOXES), 1)
@@ -306,10 +307,10 @@
     top_copy.wait_recv()
     below[...] = jnp.dot(m2x_ref[...], top[0:coeffs, :], preferred_element_type=F32)
 
-    c_copies = [send_entering(0), send_entering(1)]
+    c_copies.append(send_entering(1))
     raise_part(0)
+    add_part(0)
     c_copies.append(send_entering(2))
-    add_part(0)
     raise_part(1)
     add_part(1)
     raise_part(2)

time: 43.9 us -> 43.2 us (0.984)
  Pallas kernels: 41.7 us -> 41 us
    pallas_call x1, Pallas kernels: 41.7 us -> 41 us  [body(): pl.pallas_call(functools.partial(kernel, loop_size, layers, rows), out_sh...]
where the time goes in v4:
time: 43.2 us; the launch traced here: 43 us
  Pallas kernels  41 us (95%)
  local copies, waits for them, and re-layouts  2.03 us (5%)
    pallas_call x1, Pallas kernels, body(): pl.pallas_call(functools.partial(kernel, loop_size, layers, rows), out_sh...  41 us
    unnamed x1, local copies, waits for them, and re-layouts  2.03 us

profile of v4, /device:TPU:0, one launch (start us, length us, event | category | flops | bytes accessed | tf_op | source)
XLA Modules:
  0.0 43.0 jit_solution(2435179088061049463)
XLA Ops:
  0.0 41.0 %shard_map.82 = bf16[361,8,128]{2,1,0:T(8,128)(2,1)} custom-call(s32[2,6]{1,0:T(2,128)} %bitcast.3, bf16[361,8,128]{2,1,0:T(8,128)(2,1)} %moments_ref.1, s32[8,128]{1,0:T(8,128)} %counts_ref.1, bf16[1296,361]{1,0:T(8,128)(2,1)} %m2x_ref.1, bf16[1296,361]{1,0:T(8,128)(2,1)} %bitcast.2, f32[648]{0:T(1024)} %decay_ref.1, f32[648]{0:T(1024)} %wave_x_ref.1, ...), custom_call_target="tpu_custom_call" | custom-call | flops 7665352704 | bytes 6291456 | tf_op jit(solution)/shard_map/pallas_call | solution.py:395
  41.0 2.0 %copy.10 = bf16[361,8,128]{2,1,0:T(8,128)(2,1)} copy(bf16[361,8,128]{2,1,0:T(8,128)(2,1)} %shard_map.82) | data formatting | bytes 1478656
